TPU v7x, 32 devices: a whole 2x2x4 slice. The times are simulated.
32 devices in a mesh: dp: 2 (over core), seq: 16 (over z, y, x).
Axes of the slice: x: 2, y: 2, z: 4, core: 2. Of those that a mesh axis runs over, the one named last changes fastest.
Arguments:
- saved_mixed: bfloat16 [2, 65536, 512], P('dp', 'seq'), may hold values from -6 to 6
- out_grad: bfloat16 [2, 65536, 512], P('dp', 'seq'), may hold values from -6 to 6
- weight_in: bfloat16 [2048, 128], P('dp'), may hold values from -0.5 to 0.5
- weight_out: bfloat16 [2048, 128], P('dp'), may hold values from -0.25 to 0.25
- outer_factor: bfloat16 [256, 256], P('dp'), may hold values from -0.375 to 0.375
- inner_factor: bfloat16 [256, 256], P('dp'), may hold values from -0.375 to 0.375
- twiddle: float32 [256, 256], P(None, 'seq'), may hold values from 0.5 to 2
Outputs:
- input_grad: bfloat16 [2, 65536, 512], P('dp', 'seq')
- weight_in_grad: float32 [2048, 128], P('dp')
- weight_out_grad: float32 [2048, 128], P('dp')
All inputs are finite; a program needn't handle non-finite values.
Results may differ from a plain program's by a relative error of at most 0.0062.
Values may be sent and summed in bfloat16 or wider, within the bound.
A program may use at most 128 MiB of HBM per device.

v0:
```python
import functools
import math

import jax
import jax.numpy as jnp
from jax import lax
from jax.experimental import pallas as pl
from jax.experimental.pallas import tpu as pltpu
from jax.sharding import PartitionSpec as P

NB = 4


def dot(left, right, left_dim, right_dim):
    return lax.dot_general(
        left, right, (((left_dim,), (right_dim,)), ((), ())), preferred_element_type=jnp.float32
    )


def block_kernel(
    scale_factor, sub, saved_ref, up_ref, w_in_ref, w_out_ref, w_turn_ref, delta_ref, gin_ref, gout_ref
):
    step = pl.program_id(0)
    coeff = math.sqrt(2.0 / math.pi)

    @pl.when(step == 0)
    def _():
        gin_ref[...] = jnp.zeros_like(gin_ref)
        gout_ref[...] = jnp.zeros_like(gout_ref)

    @pl.loop(0, saved_ref.shape[0] // sub)
    def _(part):
        rows = pl.ds(pl.multiple_of(part * sub, sub), sub)
        saved = saved_ref[rows, :]
        up = up_ref[rows, :]
        pre = dot(w_in_ref[...], saved, 1, 1)
        act_grad = dot(w_out_ref[...], up, 1, 1)
        squared = pre * pre
        tangent = jnp.tanh(pre * (coeff + (coeff * 0.044715) * squared))
        half = 0.5 + 0.5 * tangent
        activated = (pre * half).astype(jnp.bfloat16)
        slope = half + (pre * (1.0 - tangent * tangent)) * (
            0.5 * coeff + (1.5 * 0.044715 * coeff) * squared
        )
        pre_grad = (act_grad * slope).astype(jnp.bfloat16)
        gout_ref[...] += dot(activated, up, 1, 0)
        gin_ref[...] += dot(pre_grad, saved, 1, 0)
        projected = dot(w_turn_ref[...], pre_grad, 1, 0)
        delta_ref[rows, :] = (up.astype(jnp.float32) + projected.T).astype(jnp.bfloat16)

    @pl.when(step == pl.num_programs(0) - 1)
    def _():
        gin_ref[...] *= scale_factor
        gout_ref[...] *= scale_factor


def block_call(block_id, scale_factor, saved, up, w_in, w_out, w_turn):
    rows, features = saved.shape
    width = features // NB
    hidden = w_in.shape[0] // NB
    tile = min(1024, rows)
    tokens = pl.BlockSpec((tile, width), lambda i: (i, block_id))
    weights = pl.BlockSpec((hidden, width), lambda i: (block_id, 0))
    total = pl.BlockSpec((hidden, width), lambda i: (0, 0))
    return pl.pallas_call(
        functools.partial(block_kernel, scale_factor, min(256, tile)),
        grid=(rows // tile,),
        in_specs=[
            tokens,
            tokens,
            weights,
            weights,
            pl.BlockSpec((width, hidden), lambda i: (0, block_id)),
        ],
        out_specs=[pl.BlockSpec((tile, width), lambda i: (i, 0)), total, total],
        out_shape=[
            jax.ShapeDtypeStruct((rows, width), jnp.bfloat16),
            jax.ShapeDtypeStruct((hidden, width), jnp.float32),
            jax.ShapeDtypeStruct((hidden, width), jnp.float32),
        ],
        compiler_params=pltpu.CompilerParams(vmem_limit_bytes=58 * 1024 * 1024),
        cost_estimate=pl.CostEstimate(
            flops=10 * rows * width * hidden,
            bytes_accessed=6 * rows * width,
            transcendentals=rows * hidden,
        ),
    )(saved, up, w_in, w_out, w_turn)


def shards(saved_mixed, out_grad, weight_in, weight_out, outer_factor, inner_factor, twiddle):
    data_devices = lax.axis_size("dp")
    seq_devices = lax.axis_size("seq")
    weight_in, weight_out, outer_factor, inner_factor = (
        lax.all_gather(weight_in, "dp", axis=0, tiled=True),
        lax.all_gather(weight_out, "dp", axis=0, tiled=True),
        lax.all_gather(outer_factor, "dp", axis=0, tiled=True),
        lax.all_gather(inner_factor, "dp", axis=0, tiled=True),
    )
    seq_count, row_count, features = saved_mixed.shape
    sub_width = features // NB
    inner_size = inner_factor.shape[0]
    local_outer = row_count // inner_size
    scale_factor = 1.0 / math.sqrt(seq_count * data_devices * row_count * seq_devices)
    saved_tokens = saved_mixed.reshape(seq_count * row_count, features)
    upstream = out_grad.reshape(seq_count * row_count, features)
    input_parts = []
    output_parts = []
    grids = []
    arrived = []
    w_turn = weight_in.T
    for block_id in range(NB):
        delta, grad_in, grad_out = block_call(
            block_id, scale_factor, saved_tokens, upstream, weight_in, weight_out, w_turn
        )
        grid = delta.reshape(seq_count, local_outer, inner_size, sub_width)
        grids.append(grid)
        arrived.append(lax.all_to_all(grid, "seq", split_axis=2, concat_axis=1, tiled=True))
        input_parts.append(grad_in)
        output_parts.append(grad_out)
    both = jnp.stack([jnp.concatenate(input_parts, axis=0), jnp.concatenate(output_parts, axis=0)])
    both = lax.psum_scatter(both, "dp", scatter_dimension=1, tiled=True)
    pieces = both.reshape(2, seq_devices, both.shape[1] // seq_devices, sub_width)
    pieces = lax.all_to_all(pieces, "seq", split_axis=1, concat_axis=1, tiled=True)
    both = lax.all_gather(jnp.sum(pieces, axis=1), "seq", axis=1, tiled=True)
    weight_in_grad, weight_out_grad = both[0], both[1]
    home = []
    for block_id in range(NB):
        outer_rows = jnp.einsum(
            "pq,spjc->sqjc",
            outer_factor,
            arrived[block_id],
            preferred_element_type=jnp.float32,
        )
        turned = (outer_rows * twiddle[None, :, :, None]).astype(jnp.bfloat16)
        home.append(lax.all_to_all(turned, "seq", split_axis=1, concat_axis=2, tiled=True))
    results = []
    for block_id in range(NB):
        back_term = jnp.einsum(
            "sipc,pj->sijc", home[block_id], inner_factor, preferred_element_type=jnp.float32
        )
        back_term = back_term.astype(jnp.bfloat16)
        results.append(
            (grids[block_id].astype(jnp.float32) + back_term.astype(jnp.float32)).astype(
                jnp.bfloat16
            )
        )
    input_grad = jnp.concatenate(results, axis=3).reshape(seq_count, row_count, features)
    return (input_grad, weight_in_grad, weight_out_grad)


def solution(mesh):
    in_specs = (
        P("dp", "seq", None),
        P("dp", "seq", None),
        P("dp", None),
        P("dp", None),
        P("dp", None),
        P("dp", None),
        P(None, "seq"),
    )
    out_specs = (P("dp", "seq", None), P("dp", None), P("dp", None))
    return jax.shard_map(shards, mesh=mesh, in_specs=in_specs, out_specs=out_specs, check_vma=False)
```

profile of v0, /device:TPU:0, one launch (start us, length us, event | category | flops | bytes accessed | tf_op | source)
XLA Modules:
  0.0 343.8 jit_solution(4001427133892478115)
XLA Ops:
  8.3 2.3 all_gather.15
  11.6 2.3 all_gather.16.w_out_ref
  13.9 13.7 %shard_map.97 = (bf16[4096,128]{1,0:T(8,128)(2,1)}, f32[512,128]{1,0:T(8,128)}, f32[512,128]{1,0:T(8,128)}) custom-call(bf16[4096,512]{1,0:T(8,128)(2,1)} %bitcast.127, bf16[4096,512]{1,0:T(8,128)(2,1)} %bitcast.131, bf16[2048,128]{1,0:T(8,128)(2,1)} %copy.84.w_in_ref, bf16[2048,128]{1,0:T(8,128)(2,1)} %all_gather.16.w_out_ref, bf16[128,2048]{1,0:T(8,128)(2,1)} %bitcast.135), custom_call_target="tpu_custom_call" | custom-call | flops 2684354560 | bytes 3145728 | tf_op jit(solution)/shard_map/pallas_call | solution.py:65
  27.6 2.9 copy.113
  30.5 8.2 %all-to-all-start.6 = ((bf16[1,16,256,128]{3,1,0,2:T(8,128)(2,1)}), bf16[1,16,256,128]{3,1,0,2:T(8,128)(2,1)S(1)}, u32[]{:S(2)}, u32[]{:S(2)}) async-start(bf16[1,16,256,128]{3,1,0,2:T(8,128)(2,1)} %copy.113), calls=%async_computation.6 | async-start | bytes 2097152 | tf_op jit(solution)/shard_map/all_to_all | solution.py:117
  38.7 13.8 %shard_map.96 = (bf16[4096,128]{1,0:T(8,128)(2,1)}, f32[512,128]{1,0:T(8,128)}, f32[512,128]{1,0:T(8,128)}) custom-call(bf16[4096,512]{1,0:T(8,128)(2,1)} %bitcast.128, bf16[4096,512]{1,0:T(8,128)(2,1)} %bitcast.132, bf16[2048,128]{1,0:T(8,128)(2,1)} %copy.84.w_in_ref, bf16[2048,128]{1,0:T(8,128)(2,1)} %all_gather.16.w_out_ref, bf16[128,2048]{1,0:T(8,128)(2,1)} %bitcast.136), custom_call_target="tpu_custom_call" | custom-call | flops 2684354560 | bytes 3145728 | tf_op jit(solution)/shard_map/pallas_call | solution.py:65
  52.5 2.9 copy.104
  55.4 7.9 %all-to-all-done.6 = bf16[1,16,256,128]{3,1,0,2:T(8,128)(2,1)S(1)} async-done(((bf16[1,16,256,128]{3,1,0,2:T(8,128)(2,1)}), bf16[1,16,256,128]{3,1,0,2:T(8,128)(2,1)S(1)}, u32[]{:S(2)}, u32[]{:S(2)}) %all-to-all-start.6) | async-done | bytes 1048608 | tf_op jit(solution)/shard_map/all_to_all | solution.py:117
  63.3 6.1 %all-to-all-start.4 = ((bf16[1,16,256,128]{3,1,0,2:T(8,128)(2,1)}), bf16[1,16,256,128]{3,1,0,2:T(8,128)(2,1)S(1)}, u32[]{:S(2)}, u32[]{:S(2)}) async-start(bf16[1,16,256,128]{3,1,0,2:T(8,128)(2,1)} %copy.104), calls=%async_computation.4 | async-start | bytes 2097152 | tf_op jit(solution)/shard_map/all_to_all | solution.py:117
  69.4 13.8 %shard_map.94 = (bf16[4096,128]{1,0:T(8,128)(2,1)}, f32[512,128]{1,0:T(8,128)}, f32[512,128]{1,0:T(8,128)}) custom-call(bf16[4096,512]{1,0:T(8,128)(2,1)} %bitcast.129, bf16[4096,512]{1,0:T(8,128)(2,1)} %bitcast.133, bf16[2048,128]{1,0:T(8,128)(2,1)} %copy.84.w_in_ref, bf16[2048,128]{1,0:T(8,128)(2,1)} %all_gather.16.w_out_ref, bf16[128,2048]{1,0:T(8,128)(2,1)} %bitcast.137), custom_call_target="tpu_custom_call" | custom-call | flops 2684354560 | bytes 3145728 | tf_op jit(solution)/shard_map/pallas_call | solution.py:65
  83.2 2.9 copy.86
  86.1 6.6 %all-to-all-done.4 = bf16[1,16,256,128]{3,1,0,2:T(8,128)(2,1)S(1)} async-done(((bf16[1,16,256,128]{3,1,0,2:T(8,128)(2,1)}), bf16[1,16,256,128]{3,1,0,2:T(8,128)(2,1)S(1)}, u32[]{:S(2)}, u32[]{:S(2)}) %all-to-all-start.4) | async-done | bytes 1048608 | tf_op jit(solution)/shard_map/all_to_all | solution.py:117
  92.7 5.9 %all-to-all-start = ((bf16[1,16,256,128]{3,1,0,2:T(8,128)(2,1)}), bf16[1,16,256,128]{3,1,0,2:T(8,128)(2,1)S(1)}, u32[]{:S(2)}, u32[]{:S(2)}) async-start(bf16[1,16,256,128]{3,1,0,2:T(8,128)(2,1)} %copy.86), calls=%async_computation | async-start | bytes 2097152 | tf_op jit(solution)/shard_map/all_to_all | solution.py:117
  98.6 13.8 %shard_map.95 = (bf16[4096,128]{1,0:T(8,128)(2,1)}, f32[512,128]{1,0:T(8,128)}, f32[512,128]{1,0:T(8,128)}) custom-call(bf16[4096,512]{1,0:T(8,128)(2,1)} %bitcast.130, bf16[4096,512]{1,0:T(8,128)(2,1)} %bitcast.134, bf16[2048,128]{1,0:T(8,128)(2,1)} %copy.84.w_in_ref, bf16[2048,128]{1,0:T(8,128)(2,1)} %all_gather.16.w_out_ref, bf16[128,2048]{1,0:T(8,128)(2,1)} %bitcast.138), custom_call_target="tpu_custom_call" | custom-call | flops 2684354560 | bytes 3145728 | tf_op jit(solution)/shard_map/pallas_call | solution.py:65
  112.4 2.9 copy.95
  115.3 6.2 %all-to-all-done = bf16[1,16,256,128]{3,1,0,2:T(8,128)(2,1)S(1)} async-done(((bf16[1,16,256,128]{3,1,0,2:T(8,128)(2,1)}), bf16[1,16,256,128]{3,1,0,2:T(8,128)(2,1)S(1)}, u32[]{:S(2)}, u32[]{:S(2)}) %all-to-all-start) | async-done | bytes 1048608 | tf_op jit(solution)/shard_map/all_to_all | solution.py:117
  121.5 6.0 %all-to-all-start.2 = ((bf16[1,16,256,128]{3,1,0,2:T(8,128)(2,1)}), bf16[1,16,256,128]{3,1,0,2:T(8,128)(2,1)S(1)}, u32[]{:S(2)}, u32[]{:S(2)}) async-start(bf16[1,16,256,128]{3,1,0,2:T(8,128)(2,1)} %copy.95), calls=%async_computation.2 | async-start | bytes 2097152 | tf_op jit(solution)/shard_map/all_to_all | solution.py:117
  127.5 1.9 all_gather.17
  130.7 1.8 copy.117
  132.5 17.9 %all-to-all-done.2 = bf16[1,16,256,128]{3,1,0,2:T(8,128)(2,1)S(1)} async-done(((bf16[1,16,256,128]{3,1,0,2:T(8,128)(2,1)}), bf16[1,16,256,128]{3,1,0,2:T(8,128)(2,1)S(1)}, u32[]{:S(2)}, u32[]{:S(2)}) %all-to-all-start.2) | async-done | bytes 1048608 | tf_op jit(solution)/shard_map/all_to_all | solution.py:117
  150.4 6.0 %all-to-all-start.7 = ((bf16[1,256,16,128]{3,2,0,1:T(8,128)(2,1)}), bf16[1,256,16,128]{3,2,0,1:T(8,128)(2,1)S(1)}, u32[]{:S(2)}, u32[]{:S(2)}) async-start(bf16[1,256,16,128]{3,2,0,1:T(8,128)(2,1)} %copy.117), calls=%async_computation.7 | async-start | bytes 2097152 | tf_op jit(solution)/shard_map/all_to_all | solution.py:135
  156.4 1.6 maximum_bitcast_fusion
  158.0 1.5 pad_maximum_fusion.1
  159.5 1.5 copy.105
  161.3 1.5 fusion.3
  162.7 2.7 copy.108
  165.4 13.8 %all-to-all-done.7 = bf16[1,256,16,128]{3,2,0,1:T(8,128)(2,1)S(1)} async-done(((bf16[1,256,16,128]{3,2,0,1:T(8,128)(2,1)}), bf16[1,256,16,128]{3,2,0,1:T(8,128)(2,1)S(1)}, u32[]{:S(2)}, u32[]{:S(2)}) %all-to-all-start.7) | async-done | bytes 1048608 | tf_op jit(solution)/shard_map/all_to_all | solution.py:135
  179.3 6.1 %all-to-all-start.5 = ((bf16[1,256,16,128]{3,2,0,1:T(8,128)(2,1)}), bf16[1,256,16,128]{3,2,0,1:T(8,128)(2,1)}, u32[]{:S(2)}, u32[]{:S(2)}) async-start(bf16[1,256,16,128]{3,2,0,1:T(8,128)(2,1)} %copy.108), calls=%async_computation.5 | async-start | bytes 2097152 | tf_op jit(solution)/shard_map/all_to_all | solution.py:135
  186.4 1.8 copy.90
  188.2 20.0 %all-to-all-done.5 = bf16[1,256,16,128]{3,2,0,1:T(8,128)(2,1)} async-done(((bf16[1,256,16,128]{3,2,0,1:T(8,128)(2,1)}), bf16[1,256,16,128]{3,2,0,1:T(8,128)(2,1)}, u32[]{:S(2)}, u32[]{:S(2)}) %all-to-all-start.5) | async-done | bytes 1048608 | tf_op jit(solution)/shard_map/all_to_all | solution.py:135
  208.3 6.0 %all-to-all-start.1 = ((bf16[1,256,16,128]{3,2,0,1:T(8,128)(2,1)}), bf16[1,256,16,128]{3,2,0,1:T(8,128)(2,1)S(1)}, u32[]{:S(2)}, u32[]{:S(2)}) async-start(bf16[1,256,16,128]{3,2,0,1:T(8,128)(2,1)} %copy.90), calls=%async_computation.1 | async-start | bytes 2097152 | tf_op jit(solution)/shard_map/all_to_all | solution.py:135
  214.3 2.3 copy.121
  216.6 20.5 %all-to-all-done.1 = bf16[1,256,16,128]{3,2,0,1:T(8,128)(2,1)S(1)} async-done(((bf16[1,256,16,128]{3,2,0,1:T(8,128)(2,1)}), bf16[1,256,16,128]{3,2,0,1:T(8,128)(2,1)S(1)}, u32[]{:S(2)}, u32[]{:S(2)}) %all-to-all-start.1) | async-done | bytes 1048608 | tf_op jit(solution)/shard_map/all_to_all | solution.py:135
  237.1 6.0 %all-to-all-start.8 = ((f32[2,16,64,128]{3,2,0,1:T(8,128)}), f32[2,16,64,128]{3,2,0,1:T(8,128)S(1)}, u32[]{:S(2)}, u32[]{:S(2)}) async-start(f32[2,16,64,128]{3,2,0,1:T(8,128)} %copy.121), calls=%async_computation.9 | async-start | bytes 2097152 | tf_op jit(solution)/shard_map/all_to_all | solution.py:123
  244.2 1.8 copy.99
  246.0 20.0 %all-to-all-done.8 = f32[2,16,64,128]{3,2,0,1:T(8,128)S(1)} async-done(((f32[2,16,64,128]{3,2,0,1:T(8,128)}), f32[2,16,64,128]{3,2,0,1:T(8,128)S(1)}, u32[]{:S(2)}, u32[]{:S(2)}) %all-to-all-start.8) | async-done | bytes 1048608 | tf_op jit(solution)/shard_map/all_to_all | solution.py:123
  266.0 6.1 %all-to-all-start.3 = ((bf16[1,256,16,128]{3,2,0,1:T(8,128)(2,1)}), bf16[1,256,16,128]{3,2,0,1:T(8,128)(2,1)}, u32[]{:S(2)}, u32[]{:S(2)}) async-start(bf16[1,256,16,128]{3,2,0,1:T(8,128)(2,1)} %copy.99), calls=%async_computation.3 | async-start | bytes 2097152 | tf_op jit(solution)/shard_map/all_to_all | solution.py:135
  272.9 1.3 copy.112
  276.0 1.5 copy.94
  277.5 1.9 all_gather.18
  279.4 2.6 copy.118
  281.9 2.5 copy.109
  285.7 9.9 %all-to-all-done.3 = bf16[1,256,16,128]{3,2,0,1:T(8,128)(2,1)} async-done(((bf16[1,256,16,128]{3,2,0,1:T(8,128)(2,1)}), bf16[1,256,16,128]{3,2,0,1:T(8,128)(2,1)}, u32[]{:S(2)}, u32[]{:S(2)}) %all-to-all-start.3) | async-done | bytes 1048608 | tf_op jit(solution)/shard_map/all_to_all | solution.py:135
  295.6 1.6 copy.100
  300.2 2.1 pad_maximum_fusion
  302.3 6.4 %copy.120 = bf16[1,16,256,512]{3,2,1,0:T(8,128)(2,1)} copy(bf16[1,16,256,512]{2,3,1,0:T(8,128)(2,1)} %pad_maximum_fusion) | data formatting | bytes 8388608 | tf_op jit(solution)/shard_map/concatenate | solution.py:147
  308.7 26.0 %all-gather.2.cloned.1.call-done = f32[2,1024,128]{2,1,0:T(8,128)} async-done(((f32[2,64,128]{2,1,0:T(8,128)}), f32[2,1024,128]{2,1,0:T(8,128)}) %all-gather.2.cloned.1.call-update) | async-done | bytes 1048592 | tf_op jit(solution)/shard_map/all_gather | solution.py:124
  334.7 2.2 slice_bitcast_fusion
  (59 shorter events, 12.5 us)
Async XLA Ops:
  7.2 4.4 %copy-start.13 = (bf16[1024,128]{1,0:T(8,128)(2,1)S(1)}, bf16[1024,128]{1,0:T(8,128)(2,1)}, u32[]{:S(2)}) copy-start(bf16[1024,128]{1,0:T(8,128)(2,1)} %param.10) | copy-start | bytes 786436
  10.6 3.3 copy-start
  30.5 32.9 %all-to-all-start.6 = ((bf16[1,16,256,128]{3,1,0,2:T(8,128)(2,1)}), bf16[1,16,256,128]{3,1,0,2:T(8,128)(2,1)S(1)}, u32[]{:S(2)}, u32[]{:S(2)}) async-start(bf16[1,16,256,128]{3,1,0,2:T(8,128)(2,1)} %copy.113), calls=%async_computation.6 | async-start | bytes 2097152 | tf_op jit(solution)/shard_map/all_to_all | solution.py:117
  63.3 29.4 %all-to-all-start.4 = ((bf16[1,16,256,128]{3,1,0,2:T(8,128)(2,1)}), bf16[1,16,256,128]{3,1,0,2:T(8,128)(2,1)S(1)}, u32[]{:S(2)}, u32[]{:S(2)}) async-start(bf16[1,16,256,128]{3,1,0,2:T(8,128)(2,1)} %copy.104), calls=%async_computation.4 | async-start | bytes 2097152 | tf_op jit(solution)/shard_map/all_to_all | solution.py:117
  92.7 19.6 %copy-start.9 = (bf16[1,16,256,128]{3,1,0,2:T(8,128)(2,1)}, bf16[1,16,256,128]{3,1,0,2:T(8,128)(2,1)S(1)}, u32[]{:S(2)}) copy-start(bf16[1,16,256,128]{3,1,0,2:T(8,128)(2,1)S(1)} %all-to-all-done.4) | copy-start | bytes 3145732
  92.7 28.8 %all-to-all-start = ((bf16[1,16,256,128]{3,1,0,2:T(8,128)(2,1)}), bf16[1,16,256,128]{3,1,0,2:T(8,128)(2,1)S(1)}, u32[]{:S(2)}, u32[]{:S(2)}) async-start(bf16[1,16,256,128]{3,1,0,2:T(8,128)(2,1)} %copy.86), calls=%async_computation | async-start | bytes 2097152 | tf_op jit(solution)/shard_map/all_to_all | solution.py:117
  112.4 15.1 %copy-start.15 = (bf16[128,256]{1,0:T(8,128)(2,1)S(1)}, bf16[128,256]{1,0:T(8,128)(2,1)}, u32[]{:S(2)}) copy-start(bf16[128,256]{1,0:T(8,128)(2,1)} %param.11) | copy-start | bytes 196612
  121.5 28.9 %all-to-all-start.2 = ((bf16[1,16,256,128]{3,1,0,2:T(8,128)(2,1)}), bf16[1,16,256,128]{3,1,0,2:T(8,128)(2,1)S(1)}, u32[]{:S(2)}, u32[]{:S(2)}) async-start(bf16[1,16,256,128]{3,1,0,2:T(8,128)(2,1)} %copy.95), calls=%async_computation.2 | async-start | bytes 2097152 | tf_op jit(solution)/shard_map/all_to_all | solution.py:117
  129.4 0.7 copy-start.12
  130.7 25.8 %copy-start.14 = (f32[512,128]{1,0:T(8,128)S(1)}, f32[512,128]{1,0:T(8,128)}, u32[]{:S(2)}) copy-start(f32[512,128]{1,0:T(8,128)} %get-tuple-element.22) | copy-start | bytes 786436
  150.4 28.9 %all-to-all-start.7 = ((bf16[1,256,16,128]{3,2,0,1:T(8,128)(2,1)}), bf16[1,256,16,128]{3,2,0,1:T(8,128)(2,1)S(1)}, u32[]{:S(2)}, u32[]{:S(2)}) async-start(bf16[1,256,16,128]{3,2,0,1:T(8,128)(2,1)} %copy.117), calls=%async_computation.7 | async-start | bytes 2097152 | tf_op jit(solution)/shard_map/all_to_all | solution.py:135
  156.4 57.9 %reduce-scatter.2.cloned.1.call-start = ((), (), s32[]{:S(2)}) async-start(), calls=%async_computation.10 | async-start | bytes 3145728 | tf_op jit(solution)/shard_map/reduce_scatter | solution.py:121
  179.3 6.4 %copy-start.8 = (bf16[1,256,16,128]{3,2,0,1:T(8,128)(2,1)}, bf16[1,256,16,128]{3,2,0,1:T(8,128)(2,1)S(1)}, u32[]{:S(2)}) copy-start(bf16[1,256,16,128]{3,2,0,1:T(8,128)(2,1)S(1)} %all-to-all-done.7) | copy-start | bytes 3145732
  179.3 29.0 %all-to-all-start.5 = ((bf16[1,256,16,128]{3,2,0,1:T(8,128)(2,1)}), bf16[1,256,16,128]{3,2,0,1:T(8,128)(2,1)}, u32[]{:S(2)}, u32[]{:S(2)}) async-start(bf16[1,256,16,128]{3,2,0,1:T(8,128)(2,1)} %copy.108), calls=%async_computation.5 | async-start | bytes 2097152 | tf_op jit(solution)/shard_map/all_to_all | solution.py:135
  208.3 28.9 %all-to-all-start.1 = ((bf16[1,256,16,128]{3,2,0,1:T(8,128)(2,1)}), bf16[1,256,16,128]{3,2,0,1:T(8,128)(2,1)S(1)}, u32[]{:S(2)}, u32[]{:S(2)}) async-start(bf16[1,256,16,128]{3,2,0,1:T(8,128)(2,1)} %copy.90), calls=%async_computation.1 | async-start | bytes 2097152 | tf_op jit(solution)/shard_map/all_to_all | solution.py:135
  237.1 6.3 %copy-start.10 = (bf16[1,256,16,128]{3,2,0,1:T(8,128)(2,1)}, bf16[1,256,16,128]{3,2,0,1:T(8,128)(2,1)S(1)}, u32[]{:S(2)}) copy-start(bf16[1,256,16,128]{3,2,0,1:T(8,128)(2,1)S(1)} %all-to-all-done.1) | copy-start | bytes 3145732
  237.1 28.9 %all-to-all-start.8 = ((f32[2,16,64,128]{3,2,0,1:T(8,128)}), f32[2,16,64,128]{3,2,0,1:T(8,128)S(1)}, u32[]{:S(2)}, u32[]{:S(2)}) async-start(f32[2,16,64,128]{3,2,0,1:T(8,128)} %copy.121), calls=%async_computation.9 | async-start | bytes 2097152 | tf_op jit(solution)/shard_map/all_to_all | solution.py:123
  246.0 26.8 %copy-start.5 = (bf16[4096,128]{1,0:T(8,128)(2,1)S(1)}, bf16[4096,128]{1,0:T(8,128)(2,1)}, u32[]{:S(2)}) copy-start(bf16[4096,128]{1,0:T(8,128)(2,1)} %get-tuple-element.18) | copy-start | bytes 3145732
  266.0 29.5 %all-to-all-start.3 = ((bf16[1,256,16,128]{3,2,0,1:T(8,128)(2,1)}), bf16[1,256,16,128]{3,2,0,1:T(8,128)(2,1)}, u32[]{:S(2)}, u32[]{:S(2)}) async-start(bf16[1,256,16,128]{3,2,0,1:T(8,128)(2,1)} %copy.99), calls=%async_computation.3 | async-start | bytes 2097152 | tf_op jit(solution)/shard_map/all_to_all | solution.py:135
  272.1 2.1 copy-start.6
  272.1 62.6 %all-gather.2.cloned.1.call-start = ((), (), s32[]{:S(2)}) async-start(), calls=%async_computation.11 | async-start | bytes 1114112 | tf_op jit(solution)/shard_map/all_gather | solution.py:124
  274.2 1.2 copy-start.7
  275.4 2.0 copy-start.16
  279.4 5.0 %copy-start.11 = (bf16[1,256,16,128]{3,2,0,1:T(8,128)(2,1)S(1)}, bf16[1,256,16,128]{3,2,0,1:T(8,128)(2,1)}, u32[]{:S(2)}) copy-start(bf16[1,256,16,128]{3,2,0,1:T(8,128)(2,1)} %copy-done.10) | copy-start | bytes 3145732
  295.6 1.7 copy-start.1
  295.6 1.9 copy-start.4
  297.2 1.3 copy-start.3
  297.9 1.3 copy-start.2
Sparse Core Ops, SparseCore 0:
  160.0 10.8 reduce-scatter.1
  276.7 58.0 all-gather.1
where the time goes:
time: 345 us; the launch traced here: 344 us
  waiting for transfers between devices  149 us (43%)
  starting transfers between devices  56.4 us (16%)
  Pallas kernels  55.1 us (16%)
  local copies, waits for them, and re-layouts  49.8 us (14%)
  between operations  14.4 us (4%)
  blocking collectives  8.36 us (2%)
  other arithmetic  5.84 us (2%)
  matrix products  4.96 us (1%)
    all_to_all x4, waiting for transfers between devices, shards(): lax.all_to_all(turned, 'seq', split_axis=1, concat_axis=2, tiled=True)  64.3 us
    pallas_call x4, Pallas kernels, block_call(): pl.pallas_call(functools.partial(block_kernel, scale_factor, min(256, til...  55.1 us
    all_to_all x4, waiting for transfers between devices, shards(): lax.all_to_all(grid, 'seq', split_axis=2, concat_axis=1, tiled=True)  38.6 us
    all_to_all x4, starting transfers between devices, shards(): lax.all_to_all(grid, 'seq', split_axis=2, concat_axis=1, tiled=True)  26.2 us
    all_gather x1, waiting for transfers between devices, shards(): both = lax.all_gather(jnp.sum(pieces, axis=1), 'seq', axis=1, tiled=True)  26 us
    all_to_all x4, starting transfers between devices, shards(): lax.all_to_all(turned, 'seq', split_axis=1, concat_axis=2, tiled=True)  24.2 us
    all_to_all x1, waiting for transfers between devices, shards(): lax.all_to_all(pieces, 'seq', split_axis=1, concat_axis=1, tiled=True)  20 us
    reshape x8, local copies, waits for them, and re-layouts, shards(): grid = delta.reshape(seq_count, local_outer, inner_size, sub_width)  15.4 us
  transfers between devices with their start and end apart: 11, of which 10 were waited for; matrix products, arithmetic and copies ran while one was open for 15% of the time, Pallas kernels for 12%

commit v1 on v0

--- a/solution.py
+++ b/solution.py
@@ -108,41 +108,41 @@
     grids = []
     arrived = []
     w_turn = weight_in.T
-    for block_id in range(NB):
-        delta, grad_in, grad_out = block_call(
-            block_id, scale_factor, saved_tokens, upstream, weight_in, weight_out, w_turn
-        )
-        grid = delta.reshape(seq_count, local_outer, inner_size, sub_width)
+    group = 2
+    for first in range(0, NB, group):
+        deltas = []
+        for block_id in range(first, first + group):
+            delta, grad_in, grad_out = block_call(
+                block_id, scale_factor, saved_tokens, upstream, weight_in, weight_out, w_turn
+            )
+            deltas.append(delta.reshape(seq_count, local_outer, inner_size, sub_width))
+            input_parts.append(grad_in)
+            output_parts.append(grad_out)
+        grid = jnp.concatenate(deltas, axis=3)
         grids.append(grid)
         arrived.append(lax.all_to_all(grid, "seq", split_axis=2, concat_axis=1, tiled=True))
-        input_parts.append(grad_in)
-        output_parts.append(grad_out)
     both = jnp.stack([jnp.concatenate(input_parts, axis=0), jnp.concatenate(output_parts, axis=0)])
     both = lax.psum_scatter(both, "dp", scatter_dimension=1, tiled=True)
+    both, arrived[0] = lax.optimization_barrier((both, arrived[0]))
     pieces = both.reshape(2, seq_devices, both.shape[1] // seq_devices, sub_width)
     pieces = lax.all_to_all(pieces, "seq", split_axis=1, concat_axis=1, tiled=True)
     both = lax.all_gather(jnp.sum(pieces, axis=1), "seq", axis=1, tiled=True)
     weight_in_grad, weight_out_grad = both[0], both[1]
     home = []
-    for block_id in range(NB):
+    for received in arrived:
         outer_rows = jnp.einsum(
-            "pq,spjc->sqjc",
-            outer_factor,
-            arrived[block_id],
-            preferred_element_type=jnp.float32,
+            "pq,spjc->sqjc", outer_factor, received, preferred_element_type=jnp.float32
         )
         turned = (outer_rows * twiddle[None, :, :, None]).astype(jnp.bfloat16)
         home.append(lax.all_to_all(turned, "seq", split_axis=1, concat_axis=2, tiled=True))
     results = []
-    for block_id in range(NB):
+    for grid, returned in zip(grids, home):
         back_term = jnp.einsum(
-            "sipc,pj->sijc", home[block_id], inner_factor, preferred_element_type=jnp.float32
+            "sipc,pj->sijc", returned, inner_factor, preferred_element_type=jnp.float32
         )
         back_term = back_term.astype(jnp.bfloat16)
         results.append(
-            (grids[block_id].astype(jnp.float32) + back_term.astype(jnp.float32)).astype(
-                jnp.bfloat16
-            )
+            (grid.astype(jnp.float32) + back_term.astype(jnp.float32)).astype(jnp.bfloat16)
         )
     input_grad = jnp.concatenate(results, axis=3).reshape(seq_count, row_count, features)
     return (input_grad, weight_in_grad, weight_out_grad)

time: 345 us -> 324 us (0.939)
  starting transfers between devices: 56.4 us -> 43.8 us
  waiting for transfers between devices: 149 us -> 139 us
  local copies, waits for them, and re-layouts: 49.8 us -> 44.3 us
  other arithmetic: 5.84 us -> 9.7 us
    reshape x8 -> x0, local copies, waits for them, and re-layouts: 15.4 us -> none  [shards(): grid = delta.reshape(seq_count, local_outer, inner_size, sub_width)]
    concatenate x0 -> x6, local copies, waits for them, and re-layouts: none -> 13.9 us  [shards(): grid = jnp.concatenate(deltas, axis=3)]
    all_gather x1, waiting for transfers between devices: 26 us -> 13.3 us  [shards(): both = lax.all_gather(jnp.sum(pieces, axis=1), 'seq', axis=1, tiled=True)]
    all_to_all x4 -> x2, starting transfers between devices: 24.2 us -> 15.6 us  [shards(): lax.all_to_all(turned, 'seq', split_axis=1, concat_axis=2, tiled=True)]
    all_to_all x4 -> x2, waiting for transfers between devices: 64.3 us -> 72.7 us  [shards(): lax.all_to_all(turned, 'seq', split_axis=1, concat_axis=2, tiled=True)]
    all_to_all x4 -> x2, starting transfers between devices: 26.2 us -> 18.4 us  [shards(): lax.all_to_all(grid, 'seq', split_axis=2, concat_axis=1, tiled=True)]
    all_to_all x1, waiting for transfers between devices: 20 us -> 14 us  [shards(): lax.all_to_all(pieces, 'seq', split_axis=1, concat_axis=1, tiled=True)]
    all_to_all x4 -> x2, local copies, waits for them, and re-layouts: 7.95 us -> 2.18 us  [shards(): lax.all_to_all(turned, 'seq', split_axis=1, concat_axis=2, tiled=True)]
  transfers between devices with their start and end apart: 11 -> 7, of which waited for: 10 -> 6; matrix products, arithmetic and copies ran while one was open for 15% -> 15% of each run, Pallas kernels for 12% -> 9%
where the time goes in v1:
time: 324 us; the launch traced here: 323 us
  waiting for transfers between devices  139 us (43%)
  Pallas kernels  55.1 us (17%)
  local copies, waits for them, and re-layouts  44.3 us (14%)
  starting transfers between devices  43.8 us (14%)
  between operations  14.4 us (4%)
  other arithmetic  9.7 us (3%)
  blocking collectives  8.36 us (3%)
  matrix products  7.8 us (2%)
    all_to_all x2, waiting for transfers between devices, shards(): lax.all_to_all(turned, 'seq', split_axis=1, concat_axis=2, tiled=True)  72.7 us
    pallas_call x4, Pallas kernels, block_call(): pl.pallas_call(functools.partial(block_kernel, scale_factor, min(256, til...  55.1 us
    all_to_all x2, waiting for transfers between devices, shards(): lax.all_to_all(grid, 'seq', split_axis=2, concat_axis=1, tiled=True)  39.3 us
    all_to_all x2, starting transfers between devices, shards(): lax.all_to_all(grid, 'seq', split_axis=2, concat_axis=1, tiled=True)  18.4 us
    all_to_all x2, starting transfers between devices, shards(): lax.all_to_all(turned, 'seq', split_axis=1, concat_axis=2, tiled=True)  15.6 us
    all_to_all x1, waiting for transfers between devices, shards(): lax.all_to_all(pieces, 'seq', split_axis=1, concat_axis=1, tiled=True)  14 us
    concatenate x6, local copies, waits for them, and re-layouts, shards(): grid = jnp.concatenate(deltas, axis=3)  13.9 us
    all_gather x1, waiting for transfers between devices, shards(): both = lax.all_gather(jnp.sum(pieces, axis=1), 'seq', axis=1, tiled=True)  13.3 us
  transfers between devices with their start and end apart: 7, of which 6 were waited for; matrix products, arithmetic and copies ran while one was open for 15% of the time, Pallas kernels for 9%

profile of v1, /device:TPU:0, one launch (start us, length us, event | category | flops | bytes accessed | tf_op | source)
XLA Modules:
  0.0 322.8 jit_solution(8700393270323689025)
XLA Ops:
  7.2 1.1 copy.45
  8.3 2.3 all_gather.15
  10.6 1.0 copy.46.w_in_ref
  11.6 2.3 all_gather.16.w_out_ref
  13.9 13.7 %shard_map.95 = (bf16[4096,128]{1,0:T(8,128)(2,1)}, f32[512,128]{1,0:T(8,128)}, f32[512,128]{1,0:T(8,128)}) custom-call(bf16[4096,512]{1,0:T(8,128)(2,1)} %bitcast.74, bf16[4096,512]{1,0:T(8,128)(2,1)} %bitcast.78, bf16[2048,128]{1,0:T(8,128)(2,1)} %copy.46.w_in_ref, bf16[2048,128]{1,0:T(8,128)(2,1)} %all_gather.16.w_out_ref, bf16[128,2048]{1,0:T(8,128)(2,1)} %bitcast.82), custom_call_target="tpu_custom_call" | custom-call | flops 2684354560 | bytes 3145728 | tf_op jit(solution)/shard_map/pallas_call | solution.py:65
  27.6 13.8 %shard_map.94 = (bf16[4096,128]{1,0:T(8,128)(2,1)}, f32[512,128]{1,0:T(8,128)}, f32[512,128]{1,0:T(8,128)}) custom-call(bf16[4096,512]{1,0:T(8,128)(2,1)} %bitcast.75, bf16[4096,512]{1,0:T(8,128)(2,1)} %bitcast.79, bf16[2048,128]{1,0:T(8,128)(2,1)} %copy.46.w_in_ref, bf16[2048,128]{1,0:T(8,128)(2,1)} %all_gather.16.w_out_ref, bf16[128,2048]{1,0:T(8,128)(2,1)} %bitcast.83), custom_call_target="tpu_custom_call" | custom-call | flops 2684354560 | bytes 3145728 | tf_op jit(solution)/shard_map/pallas_call | solution.py:65
  41.4 0.5 copy.49
  42.0 0.7 copy-done.8
  42.7 1.3 copy.48
  44.0 1.4 pad_maximum_fusion.1
  45.4 3.1 copy.52
  48.5 8.2 %all-to-all-start = ((bf16[1,16,256,256]{3,1,0,2:T(8,128)(2,1)}), bf16[1,16,256,256]{3,1,0,2:T(8,128)(2,1)S(1)}, u32[]{:S(2)}, u32[]{:S(2)}) async-start(bf16[1,16,256,256]{3,1,0,2:T(8,128)(2,1)} %copy.52), calls=%async_computation.1 | async-start | bytes 4194304 | tf_op jit(solution)/shard_map/all_to_all | solution.py:123
  56.8 13.7 %shard_map.97 = (bf16[4096,128]{1,0:T(8,128)(2,1)}, f32[512,128]{1,0:T(8,128)}, f32[512,128]{1,0:T(8,128)}) custom-call(bf16[4096,512]{1,0:T(8,128)(2,1)} %bitcast.76, bf16[4096,512]{1,0:T(8,128)(2,1)} %bitcast.80, bf16[2048,128]{1,0:T(8,128)(2,1)} %copy.46.w_in_ref, bf16[2048,128]{1,0:T(8,128)(2,1)} %all_gather.16.w_out_ref, bf16[128,2048]{1,0:T(8,128)(2,1)} %bitcast.84), custom_call_target="tpu_custom_call" | custom-call | flops 2684354560 | bytes 3145728 | tf_op jit(solution)/shard_map/pallas_call | solution.py:65
  70.6 13.8 %shard_map.96 = (bf16[4096,128]{1,0:T(8,128)(2,1)}, f32[512,128]{1,0:T(8,128)}, f32[512,128]{1,0:T(8,128)}) custom-call(bf16[4096,512]{1,0:T(8,128)(2,1)} %bitcast.77, bf16[4096,512]{1,0:T(8,128)(2,1)} %bitcast.81, bf16[2048,128]{1,0:T(8,128)(2,1)} %copy.46.w_in_ref, bf16[2048,128]{1,0:T(8,128)(2,1)} %all_gather.16.w_out_ref, bf16[128,2048]{1,0:T(8,128)(2,1)} %bitcast.85), custom_call_target="tpu_custom_call" | custom-call | flops 2684354560 | bytes 3145728 | tf_op jit(solution)/shard_map/pallas_call | solution.py:65
  84.5 1.2 maximum_bitcast_fusion
  85.7 1.5 pad_maximum_fusion.2
  87.2 1.5 copy.60
  88.7 2.6 copy.59
  91.3 2.7 pad_maximum_fusion.3
  94.0 4.8 %copy.61 = bf16[1,16,256,256]{3,1,0,2:T(8,128)(2,1)} copy(bf16[1,16,256,256]{2,3,1,0:T(8,128)(2,1)} %pad_maximum_fusion.3) | data formatting | bytes 4194304 | tf_op jit(solution)/shard_map/concatenate | solution.py:121
  98.8 1.3 all-to-all-done
  100.0 10.2 %all-to-all-start.2 = ((bf16[1,16,256,256]{3,1,0,2:T(8,128)(2,1)}), bf16[1,16,256,256]{3,1,0,2:T(8,128)(2,1)}, u32[]{:S(2)}, u32[]{:S(2)}) async-start(bf16[1,16,256,256]{3,1,0,2:T(8,128)(2,1)} %copy.61), calls=%async_computation.3 | async-start | bytes 4194304 | tf_op jit(solution)/shard_map/all_to_all | solution.py:123
  110.2 0.7 copy.53
  110.9 1.6 copy.54
  112.5 2.4 copy.69
  114.9 38.0 %all-to-all-done.2 = bf16[1,16,256,256]{3,1,0,2:T(8,128)(2,1)} async-done(((bf16[1,16,256,256]{3,1,0,2:T(8,128)(2,1)}), bf16[1,16,256,256]{3,1,0,2:T(8,128)(2,1)}, u32[]{:S(2)}, u32[]{:S(2)}) %all-to-all-start.2) | async-done | bytes 2097184 | tf_op jit(solution)/shard_map/all_to_all | solution.py:123
  152.9 9.7 %all-to-all-start.4 = ((f32[2,16,64,128]{3,2,0,1:T(8,128)}), f32[2,16,64,128]{3,2,0,1:T(8,128)S(1)}, u32[]{:S(2)}, u32[]{:S(2)}) async-start(f32[2,16,64,128]{3,2,0,1:T(8,128)} %copy.69), calls=%async_computation.5 | async-start | bytes 2097152 | tf_op jit(solution)/shard_map/all_to_all | solution.py:128
  162.7 1.9 all_gather.17
  164.6 2.3 copy.62
  167.6 1.7 fusion.1
  169.3 3.1 copy.65
  172.3 14.0 %all-to-all-done.4 = f32[2,16,64,128]{3,2,0,1:T(8,128)S(1)} async-done(((f32[2,16,64,128]{3,2,0,1:T(8,128)}), f32[2,16,64,128]{3,2,0,1:T(8,128)S(1)}, u32[]{:S(2)}, u32[]{:S(2)}) %all-to-all-start.4) | async-done | bytes 1048608 | tf_op jit(solution)/shard_map/all_to_all | solution.py:128
  186.3 5.8 %all-to-all-start.3 = ((bf16[1,256,16,256]{3,2,0,1:T(8,128)(2,1)}), bf16[1,256,16,256]{3,2,0,1:T(8,128)(2,1)S(1)}, u32[]{:S(2)}, u32[]{:S(2)}) async-start(bf16[1,256,16,256]{3,2,0,1:T(8,128)(2,1)} %copy.65), calls=%async_computation.4 | async-start | bytes 4194304 | tf_op jit(solution)/shard_map/all_to_all | solution.py:137
  192.2 4.6 %fusion.3 = bf16[1,256,16,256]{1,3,2,0:T(8,128)(2,1)} fusion(bf16[256,16,256]{2,1,0:T(8,128)(2,1)} %bitcast.90, f32[256,16]{0,1:T(8,128)S(1)} %copy-done.18, bf16[256,256]{1,0:T(8,128)(2,1)S(1)} %all_gather.17), kind=kOutput, calls=%fused_computation.8 | convolution fusion | flops 538968064 | bytes 4341760 | tf_op jit(solution)/shard_map/pq,spjc->sqjc/dot_general | solution.py:133
  196.7 4.6 %copy.56 = bf16[1,256,16,256]{3,2,0,1:T(8,128)(2,1)} copy(bf16[1,256,16,256]{1,3,2,0:T(8,128)(2,1)} %fusion.3) | data formatting | bytes 4194304 | tf_op jit(solution)/shard_map/convert_element_type | solution.py:136
  201.3 32.7 %all-to-all-done.3 = bf16[1,256,16,256]{3,2,0,1:T(8,128)(2,1)S(1)} async-done(((bf16[1,256,16,256]{3,2,0,1:T(8,128)(2,1)}), bf16[1,256,16,256]{3,2,0,1:T(8,128)(2,1)S(1)}, u32[]{:S(2)}, u32[]{:S(2)}) %all-to-all-start.3) | async-done | bytes 2097184 | tf_op jit(solution)/shard_map/all_to_all | solution.py:137
  234.0 9.8 %all-to-all-start.1 = ((bf16[1,256,16,256]{3,2,0,1:T(8,128)(2,1)}), bf16[1,256,16,256]{3,2,0,1:T(8,128)(2,1)}, u32[]{:S(2)}, u32[]{:S(2)}) async-start(bf16[1,256,16,256]{3,2,0,1:T(8,128)(2,1)} %copy.56), calls=%async_computation.2 | async-start | bytes 4194304 | tf_op jit(solution)/shard_map/all_to_all | solution.py:137
  243.9 0.7 reduce_sum.9
  244.6 1.9 all_gather.18
  246.7 1.0 copy-done.5
  248.0 0.8 fusion
  248.8 40.0 %all-to-all-done.1 = bf16[1,256,16,256]{3,2,0,1:T(8,128)(2,1)} async-done(((bf16[1,256,16,256]{3,2,0,1:T(8,128)(2,1)}), bf16[1,256,16,256]{3,2,0,1:T(8,128)(2,1)}, u32[]{:S(2)}, u32[]{:S(2)}) %all-to-all-start.1) | async-done | bytes 2097184 | tf_op jit(solution)/shard_map/all_to_all | solution.py:137
  288.8 2.0 copy.57
  291.0 0.8 fusion.2
  291.8 2.3 pad_maximum_fusion
  294.1 6.4 %copy.68 = bf16[1,16,256,512]{3,2,1,0:T(8,128)(2,1)} copy(bf16[1,16,256,512]{2,3,1,0:T(8,128)(2,1)} %pad_maximum_fusion) | data formatting | bytes 8388608 | tf_op jit(solution)/shard_map/concatenate | solution.py:147
  300.5 13.3 %all-gather.2.cloned.1.call-done = f32[2,1024,128]{2,1,0:T(8,128)} async-done(((f32[2,64,128]{2,1,0:T(8,128)}), f32[2,1024,128]{2,1,0:T(8,128)}) %all-gather.2.cloned.1.call-update) | async-done | bytes 1048592 | tf_op jit(solution)/shard_map/all_gather | solution.py:129
  313.7 2.2 slice_bitcast_fusion
  (43 shorter events, 1.6 us)
Async XLA Ops:
  7.2 4.4 %copy-start.9 = (bf16[1024,128]{1,0:T(8,128)(2,1)S(1)}, bf16[1024,128]{1,0:T(8,128)(2,1)}, u32[]{:S(2)}) copy-start(bf16[1024,128]{1,0:T(8,128)(2,1)} %param.10) | copy-start | bytes 786436
  10.6 3.3 %copy-start = (bf16[2048,128]{0,1:T(8,128)(2,1)}, bf16[2048,128]{0,1:T(8,128)(2,1)S(1)}, u32[]{:S(2)}) copy-start(bf16[2048,128]{0,1:T(8,128)(2,1)S(1)} %all_gather.15) | copy-start | bytes 1572868
  27.6 13.8 %copy-start.7 = (bf16[4096,128]{1,0:T(8,128)(2,1)S(1)}, bf16[4096,128]{1,0:T(8,128)(2,1)}, u32[]{:S(2)}) copy-start(bf16[4096,128]{1,0:T(8,128)(2,1)} %get-tuple-element.18) | copy-start | bytes 3145732
  41.4 1.2 copy-start.8
  42.0 3.4 %copy-start.1 = (bf16[1,16,256,128]{2,3,1,0:T(8,128)(2,1)}, bf16[1,16,256,128]{2,3,1,0:T(8,128)(2,1)S(1)}, u32[]{:S(2)}) copy-start(bf16[1,16,256,128]{2,3,1,0:T(8,128)(2,1)S(1)} %copy.49) | copy-start | bytes 3145732
  48.5 51.5 %all-to-all-start = ((bf16[1,16,256,256]{3,1,0,2:T(8,128)(2,1)}), bf16[1,16,256,256]{3,1,0,2:T(8,128)(2,1)S(1)}, u32[]{:S(2)}, u32[]{:S(2)}) async-start(bf16[1,16,256,256]{3,1,0,2:T(8,128)(2,1)} %copy.52), calls=%async_computation.1 | async-start | bytes 4194304 | tf_op jit(solution)/shard_map/all_to_all | solution.py:123
  56.8 55.8 %reduce-scatter.2.cloned.1.call-start = ((), (), s32[]{:S(2)}) async-start(), calls=%async_computation.6 | async-start | bytes 3145728 | tf_op jit(solution)/shard_map/reduce_scatter | solution.py:125
  70.5 13.9 %copy-start.10 = (f32[512,128]{1,0:T(8,128)S(1)}, f32[512,128]{1,0:T(8,128)}, u32[]{:S(2)}) copy-start(f32[512,128]{1,0:T(8,128)} %get-tuple-element.20) | copy-start | bytes 786436
  70.5 13.9 %copy-start.11 = (f32[512,128]{1,0:T(8,128)S(1)}, f32[512,128]{1,0:T(8,128)}, u32[]{:S(2)}) copy-start(f32[512,128]{1,0:T(8,128)} %get-tuple-element.24) | copy-start | bytes 786436
  70.6 13.9 %copy-start.12 = (f32[512,128]{1,0:T(8,128)S(1)}, f32[512,128]{1,0:T(8,128)}, u32[]{:S(2)}) copy-start(f32[512,128]{1,0:T(8,128)} %get-tuple-element.19) | copy-start | bytes 786436
  70.6 13.9 %copy-start.13 = (f32[512,128]{1,0:T(8,128)S(1)}, f32[512,128]{1,0:T(8,128)}, u32[]{:S(2)}) copy-start(f32[512,128]{1,0:T(8,128)} %get-tuple-element.23) | copy-start | bytes 786436
  70.6 13.9 %copy-start.14 = (f32[512,128]{1,0:T(8,128)S(1)}, f32[512,128]{1,0:T(8,128)}, u32[]{:S(2)}) copy-start(f32[512,128]{1,0:T(8,128)} %get-tuple-element.22) | copy-start | bytes 786436
  70.6 13.9 %copy-start.15 = (f32[512,128]{1,0:T(8,128)S(1)}, f32[512,128]{1,0:T(8,128)}, u32[]{:S(2)}) copy-start(f32[512,128]{1,0:T(8,128)} %get-tuple-element.26) | copy-start | bytes 786436
  88.6 5.4 %copy-start.4 = (bf16[1,16,256,128]{2,3,1,0:T(8,128)(2,1)}, bf16[1,16,256,128]{2,3,1,0:T(8,128)(2,1)S(1)}, u32[]{:S(2)}) copy-start(bf16[1,16,256,128]{2,3,1,0:T(8,128)(2,1)S(1)} %copy.60) | copy-start | bytes 3145732
  100.0 52.9 %all-to-all-start.2 = ((bf16[1,16,256,256]{3,1,0,2:T(8,128)(2,1)}), bf16[1,16,256,256]{3,1,0,2:T(8,128)(2,1)}, u32[]{:S(2)}, u32[]{:S(2)}) async-start(bf16[1,16,256,256]{3,1,0,2:T(8,128)(2,1)} %copy.61), calls=%async_computation.3 | async-start | bytes 4194304 | tf_op jit(solution)/shard_map/all_to_all | solution.py:123
  112.5 50.1 %copy-start.16 = (bf16[128,256]{1,0:T(8,128)(2,1)S(1)}, bf16[128,256]{1,0:T(8,128)(2,1)}, u32[]{:S(2)}) copy-start(bf16[128,256]{1,0:T(8,128)(2,1)} %param.11) | copy-start | bytes 196612
  152.9 33.4 %all-to-all-start.4 = ((f32[2,16,64,128]{3,2,0,1:T(8,128)}), f32[2,16,64,128]{3,2,0,1:T(8,128)S(1)}, u32[]{:S(2)}, u32[]{:S(2)}) async-start(f32[2,16,64,128]{3,2,0,1:T(8,128)} %copy.69), calls=%async_computation.5 | async-start | bytes 2097152 | tf_op jit(solution)/shard_map/all_to_all | solution.py:128
  166.9 0.7 copy-start.18
  186.3 47.7 %all-to-all-start.3 = ((bf16[1,256,16,256]{3,2,0,1:T(8,128)(2,1)}), bf16[1,256,16,256]{3,2,0,1:T(8,128)(2,1)S(1)}, u32[]{:S(2)}, u32[]{:S(2)}) async-start(bf16[1,256,16,256]{3,2,0,1:T(8,128)(2,1)} %copy.65), calls=%async_computation.4 | async-start | bytes 4194304 | tf_op jit(solution)/shard_map/all_to_all | solution.py:137
  201.3 43.3 %copy-start.17 = (bf16[128,256]{1,0:T(8,128)(2,1)S(1)}, bf16[128,256]{1,0:T(8,128)(2,1)}, u32[]{:S(2)}) copy-start(bf16[128,256]{1,0:T(8,128)(2,1)} %param.12) | copy-start | bytes 196612
  234.0 54.8 %all-to-all-start.1 = ((bf16[1,256,16,256]{3,2,0,1:T(8,128)(2,1)}), bf16[1,256,16,256]{3,2,0,1:T(8,128)(2,1)}, u32[]{:S(2)}, u32[]{:S(2)}) async-start(bf16[1,256,16,256]{3,2,0,1:T(8,128)(2,1)} %copy.56), calls=%async_computation.2 | async-start | bytes 4194304 | tf_op jit(solution)/shard_map/all_to_all | solution.py:137
  243.8 69.9 %all-gather.2.cloned.1.call-start = ((), (), s32[]{:S(2)}) async-start(), calls=%async_computation.7 | async-start | bytes 1114112 | tf_op jit(solution)/shard_map/all_gather | solution.py:129
  246.5 1.2 copy-start.5
  246.5 1.5 copy-start.6
  288.8 2.0 copy-start.2
  288.8 2.2 copy-start.3
Sparse Core Ops, SparseCore 0:
  87.3 10.8 reduce-scatter.1
  248.4 65.3 all-gather.1
